TPU v7x, 1024 devices: a whole 4x4x32 slice. The times are simulated.
1024 devices in a mesh: grp: 16 (over x, y), own: 64 (over z, core).
Axes of the slice: x: 4, y: 4, z: 32, core: 2. Of those that a mesh axis runs over, the one named last changes fastest.
Arguments:
- user_factors: bfloat16 [4194304, 128], P(('grp', 'own')), as said below
- user_rows: int32 [6291456], P(('grp', 'own')), may hold values from 0 to 4095
- row_counts: int32 [1048576], P(('grp', 'own')), may hold values from 1 to 6, as said below
- confidence: bfloat16 [6291456], P(('grp', 'own')), may hold values from 50 to 1000
- slot_items: int32 [1024], replicated, may hold values from 0 to 1023, each once
- prev_factors: float32 [64, 16, 128], P('own', 'grp'), may hold values from -6 to 6
Outputs:
- item_factors: float32 [64, 16, 128], P('own', 'grp')
Inputs may be any that keep to these rules, and one draw needn't show every extreme that they name: `user_factors`: each device holds a block of user factor rows; rows and columns differ in scale. `user_rows`: a local row of the same device's block of 4096 users; slots at or beyond the item's count are not used. `row_counts`: some items use all 6 slots on every device.
All inputs are finite; a program needn't handle non-finite values.
Results may differ from a plain program's by a relative error of at most 0.0003.
The roundings to bfloat16 on the way count: a program that leaves them out, or rounds other values in their place, can miss the bound.
Values may be sent and summed in bfloat16 or wider, within the bound.
A program may use at most 32 MiB of HBM per device.

v0:
```python
import jax
import jax.numpy as jnp
from jax import lax
from jax.sharding import PartitionSpec as P

CG_STEPS = 3


RIDGE = 4.0
EPSILON = 1e-06


def conjugate(system, rhs, start):

    def applied_to(vector):
        return jnp.einsum("ikl,il->ik", system, vector, precision=lax.Precision.HIGHEST)

    answer = start
    residual = rhs - applied_to(start)
    direction = residual
    norm_now = jnp.sum(residual * residual, axis=1)
    for step in range(CG_STEPS):
        applied = applied_to(direction)
        step_size = norm_now / (jnp.sum(direction * applied, axis=1) + EPSILON)
        answer = answer + step_size[:, None] * direction
        residual = residual - step_size[:, None] * applied
        norm_next = jnp.sum(residual * residual, axis=1)
        direction = residual + (norm_next / (norm_now + EPSILON))[:, None] * direction
        norm_now = norm_next
    return answer


def item_terms(factor_rows, conf_rows):
    conf_values = conf_rows.astype(jnp.float32)
    scaled = (conf_values[..., None] * factor_rows.astype(jnp.float32)).astype(jnp.bfloat16)
    weight = (1.0 + conf_values).astype(jnp.bfloat16)
    item_gram = jnp.einsum("irk,irl->ikl", scaled, factor_rows, preferred_element_type=jnp.float32)
    rhs = jnp.einsum("ir,irk->ik", weight, factor_rows, preferred_element_type=jnp.float32)
    return (item_gram, rhs)


def on_device(user_factors, user_rows, row_counts, confidence, slot_items, prev_factors):
    rank_width = user_factors.shape[1]
    window = row_counts.shape[0]
    depth = user_rows.shape[0] // window
    owners = lax.axis_size("own")
    groups = lax.axis_size("grp")
    per_device = prev_factors.shape[1]
    per_owner = per_device * groups
    local_gram = lax.dot_general(
        user_factors, user_factors, (((0,), (0,)), ((), ())), preferred_element_type=jnp.float32
    )
    picked = jnp.take(user_rows.reshape(window, depth), slot_items, axis=0)
    counts = jnp.take(row_counts, slot_items)
    conf_rows = jnp.take(confidence.reshape(window, depth), slot_items, axis=0)
    is_live = lax.broadcasted_iota(jnp.int32, (window, depth), 1) < counts[:, None]
    gathered = jnp.take(user_factors, picked.reshape(-1), axis=0).reshape(window, depth, rank_width)
    masked = jnp.where(is_live[:, :, None], gathered, jnp.zeros_like(gathered))
    identity = jnp.eye(rank_width, dtype=jnp.float32)
    outgoing = masked.reshape(owners, per_owner, depth, rank_width)
    conf_out = conf_rows.reshape(owners, per_owner, depth)
    got_rows, got_conf = (
        lax.all_to_all(outgoing, "own", split_axis=0, concat_axis=2, tiled=True),
        lax.all_to_all(conf_out, "own", split_axis=0, concat_axis=2, tiled=True),
    )
    item_gram, rhs_part = item_terms(got_rows[0], got_conf[0])
    user_gram = lax.psum(local_gram, ("grp", "own"))
    gram_part, rhs = (
        lax.psum_scatter(item_gram, "grp", scatter_dimension=0, tiled=True),
        lax.psum_scatter(rhs_part, "grp", scatter_dimension=0, tiled=True),
    )
    system = gram_part + user_gram[None] + RIDGE * identity[None]
    answer = conjugate(system, rhs, prev_factors[0])
    return answer.reshape(1, per_device, rank_width)


def solution(mesh):
    in_specs = (
        P(("grp", "own"), None),
        P(("grp", "own")),
        P(("grp", "own")),
        P(("grp", "own")),
        P(),
        P("own", "grp", None),
    )
    out_specs = P("own", "grp", None)
    return jax.shard_map(
        on_device, mesh=mesh, in_specs=in_specs, out_specs=out_specs, check_vma=False
    )
```

profile of v0, /device:TPU:6, one launch (start us, length us, event | category | flops | bytes accessed | tf_op | source)
XLA Modules:
  0.0 1017.0 jit_solution(8093382915685942542)
XLA Ops:
  7.4 0.8 fusion.13
  8.2 4.5 gather_fusion.1
  12.8 0.5 reshape.193
  13.4 3.2 gather_fusion
  16.6 0.5 copy.17
  17.1 0.7 broadcast_select_fusion.1
  17.8 29.4 %all-to-all-start = ((bf16[64,16,6]{1,2,0:T(8,128)(2,1)}), bf16[64,16,6]{1,2,0:T(8,128)(2,1)S(1)}, u32[]{:S(2)}, u32[]{:S(2)}) async-start(bf16[64,16,6]{1,2,0:T(8,128)(2,1)} %broadcast_select_fusion.1), calls=%async_computation | async-start | bytes 262144 | tf_op jit(solution)/shard_map/all_to_all | solution.py:64
  47.4 0.5 reshape.194
  47.9 2.8 gather_fusion.2
  50.9 0.4 copy.18
  51.5 0.5 copy.19
  52.4 22.1 %gather_fusion.3 = bf16[6144,128]{1,0:T(8,128)(2,1)} fusion(bf16[4096,128]{1,0:T(8,128)(2,1)S(1)} %copy-done, s32[6144]{0:T(1024)S(1)} %broadcast_clamp_fusion), kind=kCustom, calls=%fused_computation.3 | custom fusion | bytes 3170304 | tf_op jit(solution)/shard_map/jit(_take)/gather | solution.py:57
  74.5 2.4 gather.28
  77.0 2.8 select_select_fusion
  79.8 1.5 copy.20
  81.2 22.3 %all-to-all-start.1 = ((bf16[64,16,6,128]{3,1,2,0:T(8,128)(2,1)}), bf16[64,16,6,128]{3,1,2,0:T(8,128)(2,1)S(1)}, u32[]{:S(2)}, u32[]{:S(2)}) async-start(bf16[64,16,6,128]{3,1,2,0:T(8,128)(2,1)} %copy.20), calls=%async_computation.1 | async-start | bytes 3145728 | tf_op jit(solution)/shard_map/all_to_all | solution.py:63
  103.6 1.1 convolution_bitcast_fusion
  104.8 155.3 %all-to-all-done.1 = bf16[64,16,6,128]{3,1,2,0:T(8,128)(2,1)S(1)} async-done(((bf16[64,16,6,128]{3,1,2,0:T(8,128)(2,1)}), bf16[64,16,6,128]{3,1,2,0:T(8,128)(2,1)S(1)}, u32[]{:S(2)}, u32[]{:S(2)}) %all-to-all-start.1) | async-done | bytes 1572896 | tf_op jit(solution)/shard_map/all_to_all | solution.py:63
  260.1 1.0 multiply_convert_fusion
  261.1 2.2 fusion
  263.3 1.3 dynamic-slice
  264.8 0.5 fusion.2
  265.3 34.6 %all-reduce = f32[16,128]{1,0:T(8,128)S(1)} all-reduce(f32[16,128]{1,0:T(8,128)S(1)} %bitcast.93), channel_id=2, replica_groups=mesh['grp'=16,'own'=64] {'grp'}, use_global_device_ids=true, to_apply=%region_0.1.clone | all-reduce | flops 2048 | bytes 16384
  299.9 696.8 %all-reduce.4.cloned.1.call-done = f32[1,128,128]{2,1,0:T(8,128)} async-done(((f32[1,128,128]{2,1,0:T(8,128)}), f32[1,128,128]{2,1,0:T(8,128)}) %all-reduce.4.cloned.1.call-update) | async-done | bytes 65552 | tf_op jit(solution)/shard_map/psum | solution.py:67
  996.7 0.9 select_add_fusion
  997.6 0.8 convolution_subtract_fusion
  998.4 0.9 multiply_reduce_fusion.3
  1001.4 0.6 multiply_reduce_fusion.2
  1003.3 0.9 multiply_reduce_fusion.1
  1005.6 0.6 multiply_reduce_fusion
  1006.8 0.9 fusion.5
  1009.1 0.5 fusion.20
  (32 shorter events, 1.4 us)
Async XLA Ops:
  7.4 45.1 %copy-start = (bf16[4096,128]{1,0:T(8,128)(2,1)S(1)}, bf16[4096,128]{1,0:T(8,128)(2,1)}, u32[]{:S(2)}) copy-start(bf16[4096,128]{1,0:T(8,128)(2,1)} %param.6) | copy-start | bytes 3145732
  7.4 0.8 copy-start.1
  8.2 4.6 copy-start.3
  8.2 4.7 copy-start.4
  13.4 34.0 %copy-start.2 = (s32[6144]{0:T(1024)S(1)}, s32[6144]{0:T(1024)}, u32[]{:S(2)}) copy-start(s32[6144]{0:T(1024)} %param.7) | copy-start | bytes 73732
  17.8 63.5 %all-to-all-start = ((bf16[64,16,6]{1,2,0:T(8,128)(2,1)}), bf16[64,16,6]{1,2,0:T(8,128)(2,1)S(1)}, u32[]{:S(2)}, u32[]{:S(2)}) async-start(bf16[64,16,6]{1,2,0:T(8,128)(2,1)} %broadcast_select_fusion.1), calls=%async_computation | async-start | bytes 262144 | tf_op jit(solution)/shard_map/all_to_all | solution.py:64
  81.2 178.9 %all-to-all-start.1 = ((bf16[64,16,6,128]{3,1,2,0:T(8,128)(2,1)}), bf16[64,16,6,128]{3,1,2,0:T(8,128)(2,1)S(1)}, u32[]{:S(2)}, u32[]{:S(2)}) async-start(bf16[64,16,6,128]{3,1,2,0:T(8,128)(2,1)} %copy.20), calls=%async_computation.1 | async-start | bytes 3145728 | tf_op jit(solution)/shard_map/all_to_all | solution.py:63
  103.5 893.1 %all-reduce.4.cloned.1.call-start = ((), (), s32[]{:S(2)}) async-start(), calls=%async_computation.3 | async-start | bytes 131072 | tf_op jit(solution)/shard_map/psum | solution.py:67
  104.7 892.0 %reduce-scatter.4.cloned.1.call-start = ((), (), s32[]{:S(2)}) async-start(), calls=%async_computation.4 | async-start | bytes 1114112
  263.3 734.3 %copy-start.5 = (f32[1,1,128]{2,1,0:T(1,128)S(1)}, f32[1,1,128]{2,1,0:T(1,128)}, u32[]{:S(2)}) copy-start(f32[1,1,128]{2,1,0:T(1,128)} %param.11) | copy-start | bytes 1540
Sparse Core Ops, SparseCore 0:
  110.7 885.9 all-reduce.3
Sparse Core Ops, SparseCore 1:
  263.4 89.9 reduce-scatter.3
where the time goes:
time: 1020 us
  waiting for transfers between devices  852 us (84%)
  starting transfers between devices  51.7 us (5%)
  local copies, waits for them, and re-layouts  40.9 us (4%)
  blocking collectives  34.6 us (3%)
  between operations  21.8 us (2%)
    psum x1, waiting for transfers between devices, on_device(): user_gram = lax.psum(local_gram, ('grp', 'own'))  697 us
    all_to_all x1, waiting for transfers between devices, on_device(): lax.all_to_all(outgoing, 'own', split_axis=0, concat_axis=2, tiled=True)  155 us
    unnamed x1, blocking collectives  34.6 us
    all_to_all x1, starting transfers between devices, on_device(): lax.all_to_all(conf_out, 'own', split_axis=0, concat_axis=2, tiled=True)  29.4 us
    gather x2, local copies, waits for them, and re-layouts, on_device(): jnp.take(user_factors, picked.reshape(-1), axis=0)  24.5 us
    all_to_all x1, starting transfers between devices, on_device(): lax.all_to_all(outgoing, 'own', split_axis=0, concat_axis=2, tiled=True)  22.3 us
  transfers between devices with their start and end apart: 4, of which 2 were waited for; matrix products, arithmetic and copies ran while one was open for 4% of the time, Pallas kernels for 0%

commit v1 on v0

v1 whole, which is shorter than its diff:
```python
import functools

import jax
import jax.numpy as jnp
from jax import lax
from jax.experimental import pallas as pl
from jax.experimental.pallas import tpu as pltpu
from jax.sharding import PartitionSpec as P

CG_STEPS = 3
RIDGE = 4.0
EPSILON = 1e-06

RANK = 128
DEPTH = 6
USERS = 4096
WINDOW = 1024
SIDE = 4
PLANES = 32
PEERS = 32
CHUNKS = 4
GROUP = PLANES // CHUNKS
STEPS = PLANES // 2
ROWS = GROUP * DEPTH
HALF = RANK // 2
BODY = RANK
UNIT = 136
SLICE = 8
MESH = pl.DeviceIdType.MESH


def place():
    grp = lax.axis_index("grp")
    own = lax.axis_index("own")
    return grp // SIDE, grp % SIDE, own // 2, own % 2


def peer(step):
    gx, gy, z, core = place()
    px = (gx + (step // 2) % SIDE) % SIDE
    py = (gy + step // (2 * SIDE)) % SIDE
    pc = (core + step % 2) % 2
    grp = px * SIDE + py
    return pc * 16 + grp, (grp, z * 2 + pc)


def neighbour(step):
    _, _, z, core = place()
    return (lax.axis_index("grp"), ((z + step + PLANES) % PLANES) * 2 + core)


def plane_of(chunk, index):
    z = lax.axis_index("own") // 2
    step = chunk * (GROUP // 2) + index // 2
    away = STEPS - step if index % 2 == 0 else step - (STEPS - 1)
    return (z + away + PLANES) % PLANES


def solve(system, rhs, start):
    row = lax.broadcasted_iota(jnp.int32, (RANK, RANK), 0)
    col = lax.broadcasted_iota(jnp.int32, (RANK, RANK), 1)
    same = row == col

    def applied_to(vector):
        column = jnp.sum(system * vector, axis=1, keepdims=True)
        return jnp.sum(jnp.where(same, column, 0.0), axis=0, keepdims=True)

    answer = start
    residual = rhs - applied_to(start)
    direction = residual
    norm_now = jnp.sum(residual * residual, axis=1, keepdims=True)
    for step in range(CG_STEPS):
        applied = applied_to(direction)
        step_size = norm_now / (jnp.sum(direction * applied, axis=1, keepdims=True) + EPSILON)
        answer = answer + step_size * direction
        residual = residual - step_size * applied
        norm_next = jnp.sum(residual * residual, axis=1, keepdims=True)
        direction = residual + (norm_next / (norm_now + EPSILON)) * direction
        norm_now = norm_next
    return answer


def kernel(
    items, rows, conf, users, start, out,
    wide, stage, send, recv, flat, conf_wide, conf_stage, conf_send, conf_recv, conf_all, weight_all,
    gram_own, gram_pair, gram_parts, gram_piece, gram_sum, gram_pack, up_send, up_recv, down_send, down_recv,
    send_sem, recv_sem, self_sem, conf_send_sem, conf_recv_sem, conf_self_sem, pair_sem, part_sem, sum_sem,
    up_send_sem, up_recv_sem, down_send_sem, down_recv_sem,
):
    gx, gy, z, core = place()
    grp = gx * SIDE + gy
    me = core * 16 + grp
    barrier = pltpu.get_barrier_semaphore()

    def greet(step, carry):
        pl.semaphore_signal(barrier, inc=1, device_id=peer(step)[1], device_id_type=MESH)
        return carry

    lax.fori_loop(1, PEERS, greet, 0)
    for step in (1, -1):
        pl.semaphore_signal(barrier, inc=1, device_id=neighbour(step), device_id_type=MESH)

    gram_own[...] = jnp.zeros_like(gram_own)

    def own_gram(block, carry):
        at = pl.ds(pl.multiple_of(block * 512, 512), 512)
        part = users[at, :]
        wide[at, :] = part.astype(jnp.float32)
        gram_own[...] += lax.dot_general(part, part, (((0,), (0,)), ((), ())), preferred_element_type=jnp.float32)
        return carry

    lax.fori_loop(0, USERS // 512, own_gram, 0)

    spread_row = lax.broadcasted_iota(jnp.int32, (8, RANK), 0)
    spread_col = lax.broadcasted_iota(jnp.int32, (8, RANK), 1)
    mine = (spread_col // 8) % 8 == me % 8
    spread = jnp.where(jnp.logical_and(mine, spread_col % 8 == spread_row), 1.0, 0.0).astype(jnp.bfloat16)
    conf_wide[...] = jnp.dot(conf[...], spread, preferred_element_type=jnp.float32)

    for index in range(16):
        flat[pl.ds(index * 128, 128), :] = jnp.zeros((128, RANK), jnp.float32)

    pl.semaphore_wait(barrier, PEERS + 1)

    pair = pltpu.make_async_remote_copy(
        src_ref=gram_own, dst_ref=gram_pair, send_sem=pair_sem.at[0], recv_sem=pair_sem.at[1],
        device_id=(grp, z * 2 + (1 - core)), device_id_type=MESH,
    )
    pair.start()

    def gather(chunk):
        planes = [plane_of(chunk, index) for index in range(GROUP)]

        def owner(to, carry):
            for index in range(GROUP):
                item = items[planes[index] * PEERS + to]
                for slot in range(DEPTH):
                    row = rows[item * DEPTH + slot]
                    stage[pl.ds(to * ROWS + slot * GROUP + index, 1), :] = wide[pl.ds(row, 1), :]
                conf_stage[pl.ds(to * PLANES + chunk * GROUP + index, 1), :] = conf_wide[pl.ds(item, 1), :]
            return carry

        lax.fori_loop(0, PEERS, owner, 0)

        def narrow(block, carry):
            at = pl.ds(pl.multiple_of(block * ROWS * 4, ROWS * 4), ROWS * 4)
            part = stage[at, :].astype(jnp.bfloat16)
            send[chunk, pl.ds(block * 4, 4)] = part.reshape(4, ROWS, RANK)
            return carry

        lax.fori_loop(0, PEERS // 4, narrow, 0)

    def post(chunk):
        def one(step, carry):
            to, device = peer(step)
            pltpu.make_async_remote_copy(
                src_ref=send.at[chunk, to], dst_ref=recv.at[chunk, me], send_sem=send_sem.at[chunk],
                recv_sem=recv_sem.at[chunk], device_id=device, device_id_type=MESH,
            ).start()
            return carry

        lax.fori_loop(1, PEERS, one, 0)
        pltpu.make_async_copy(send.at[chunk, me], recv.at[chunk, me], self_sem.at[chunk]).start()

    def post_conf():
        left = lax.broadcasted_iota(jnp.int32, (16, RANK), 1) < HALF

        def narrow(to, carry):
            first = conf_stage[pl.ds(to * PLANES, 16), :]
            second = conf_stage[pl.ds(to * PLANES + 16, 16), :]
            conf_send[to] = jnp.where(left, first, second).astype(jnp.bfloat16)
            return carry

        lax.fori_loop(0, PEERS, narrow, 0)

        def one(step, carry):
            to, device = peer(step)
            pltpu.make_async_remote_copy(
                src_ref=conf_send.at[to], dst_ref=conf_recv.at[me], send_sem=conf_send_sem,
                recv_sem=conf_recv_sem, device_id=device, device_id_type=MESH,
            ).start()
            return carry

        lax.fori_loop(1, PEERS, one, 0)
        pltpu.make_async_copy(conf_send.at[me], conf_recv.at[me], conf_self_sem).start()

    def take_conf():
        pltpu.make_async_copy(
            conf_recv.at[pl.ds(0, PEERS - 1)], conf_recv.at[pl.ds(0, PEERS - 1)], conf_recv_sem
        ).wait()
        pltpu.make_async_copy(conf_send.at[me], conf_recv.at[me], conf_self_sem).wait()
        left = lax.broadcasted_iota(jnp.int32, (16, RANK), 1) < HALF
        sums = []
        for part in range(4):
            total = jnp.zeros((16, RANK), jnp.float32)
            for index in range(8):
                total = total + conf_recv[part * 8 + index].astype(jnp.float32)
            sums.append(total)
        for part in range(2):
            one, two = sums[2 * part], sums[2 * part + 1]
            first = jnp.where(left, one, pltpu.roll(two, HALF, 1))
            second = jnp.where(left, pltpu.roll(one, HALF, 1), two)
            at = pl.ds(part * RANK, RANK)
            conf_all[pl.ds(0, 16), at] = first
            conf_all[pl.ds(16, 16), at] = second
        values = conf_all[...]
        weight = (1.0 + values).astype(jnp.bfloat16).astype(jnp.float32)
        weight_all[...] = jnp.where(values > 0.0, weight, 0.0)

    def sum_pair():
        pair.wait()
        gram_own[...] += gram_pair[...]

    def post_parts():
        def one(step, carry):
            px = (gx + step % SIDE) % SIDE
            py = (gy + step // SIDE) % SIDE
            to = px * SIDE + py
            pltpu.make_async_remote_copy(
                src_ref=gram_own.at[pl.ds(to * SLICE, SLICE)], dst_ref=gram_parts.at[grp], send_sem=part_sem.at[0],
                recv_sem=part_sem.at[1], device_id=(to, z * 2 + core), device_id_type=MESH,
            ).start()
            return carry

        lax.fori_loop(1, 16, one, 0)
        gram_parts[grp] = gram_own[pl.ds(pl.multiple_of(grp * SLICE, SLICE), SLICE), :]

    def wait_fifteen(ref, sem):
        pltpu.make_async_copy(ref.at[pl.ds(0, 15)], ref.at[pl.ds(0, 15)], sem).wait()

    def post_sums():
        wait_fifteen(gram_parts, part_sem.at[1])
        total = gram_parts[0]
        for index in range(1, 16):
            total = total + gram_parts[index]
        gram_piece[...] = total

        def one(step, carry):
            px = (gx + step % SIDE) % SIDE
            py = (gy + step // SIDE) % SIDE
            to = px * SIDE + py
            pltpu.make_async_remote_copy(
                src_ref=gram_piece, dst_ref=gram_sum.at[grp], send_sem=sum_sem.at[0],
                recv_sem=sum_sem.at[1], device_id=(to, z * 2 + core), device_id_type=MESH,
            ).start()
            return carry

        lax.fori_loop(1, 16, one, 0)
        gram_sum[grp] = total

    def take_sums():
        wait_fifteen(gram_sum, sum_sem.at[1])
        gram_pack[pl.ds(0, BODY), :] = gram_sum[...].reshape(RANK, RANK)
        gram_pack[pl.ds(BODY, 8), :] = jnp.zeros((8, RANK), jnp.float32)

    def item_pack(into, chunk, index):
        values = flat[pl.ds(index, PEERS * 8, stride=GROUP), :]
        conf_row = conf_all[pl.ds(chunk * GROUP + index, 1), :]
        weight = weight_all[pl.ds(chunk * GROUP + index, 1), :]
        scaled = (jnp.transpose(values) * conf_row).astype(jnp.bfloat16)
        weights = jnp.broadcast_to(weight, (16, PEERS * 8)).astype(jnp.bfloat16)
        left = jnp.concatenate([scaled, weights], axis=0)
        product = jnp.dot(left, values.astype(jnp.bfloat16), preferred_element_type=jnp.float32)
        into[pl.ds(0, BODY), :] = product[:BODY] + gram_pack[pl.ds(0, BODY), :]
        into[pl.ds(BODY, 8), :] = product[BODY:BODY + 8]

    def up_copy(step):
        return pltpu.make_async_remote_copy(
            src_ref=up_send.at[step], dst_ref=up_recv.at[step], send_sem=up_send_sem.at[step],
            recv_sem=up_recv_sem.at[step], device_id=neighbour(1), device_id_type=MESH,
        )

    def down_copy(step):
        return pltpu.make_async_remote_copy(
            src_ref=down_send.at[step], dst_ref=down_recv.at[step], send_sem=down_send_sem.at[step],
            recv_sem=down_recv_sem.at[step], device_id=neighbour(-1), device_id_type=MESH,
        )

    gather(0)
    post(0)
    sum_pair()
    post_parts()
    gather(1)
    post(1)
    post_sums()
    gather(2)
    post(2)
    gather(3)
    post_conf()
    post(3)
    take_sums()
    take_conf()

    def chain(step, carry):
        chunk = step // (GROUP // 2)
        index = (step % (GROUP // 2)) * 2

        @pl.when(index == 0)
        def _():
            pltpu.make_async_copy(
                recv.at[chunk, pl.ds(0, PEERS - 1)], recv.at[chunk, pl.ds(0, PEERS - 1)], recv_sem.at[chunk]
            ).wait()
            pltpu.make_async_copy(send.at[chunk, me], recv.at[chunk, me], self_sem.at[chunk]).wait()

            def widen(source, carry):
                at = pl.ds(pl.multiple_of(source * 64, 64), ROWS)
                flat[at, :] = recv[chunk, source].astype(jnp.float32)
                return carry

            lax.fori_loop(0, PEERS, widen, 0)

        item_pack(up_send.at[step], chunk, index)
        item_pack(down_send.at[step], chunk, index + 1)

        @pl.when(step > 0)
        def _():
            up_copy(step - 1).wait_recv()
            up_send[step] += up_recv[step - 1]
            down_copy(step - 1).wait_recv()
            down_send[step] += down_recv[step - 1]

        up_copy(step).start()

        @pl.when(step < STEPS - 1)
        def _():
            down_copy(step).start()

        return carry

    lax.fori_loop(0, STEPS, chain, 0)
    up_copy(STEPS - 1).wait_recv()
    total = down_send[STEPS - 1] + up_recv[STEPS - 1]
    row = lax.broadcasted_iota(jnp.int32, (RANK, RANK), 0)
    col = lax.broadcasted_iota(jnp.int32, (RANK, RANK), 1)
    system = total[:BODY] + jnp.where(row == col, RIDGE, 0.0)
    out[0] = solve(system, total[BODY:BODY + 1], start[0])

    for chunk in range(CHUNKS):
        pltpu.make_async_copy(
            send.at[chunk, pl.ds(0, PEERS - 1)], send.at[chunk, pl.ds(0, PEERS - 1)], send_sem.at[chunk]
        ).wait()
    pltpu.make_async_copy(
        conf_send.at[pl.ds(0, PEERS - 1)], conf_send.at[pl.ds(0, PEERS - 1)], conf_send_sem
    ).wait()
    wait_fifteen(gram_parts, part_sem.at[0])
    wait_fifteen(gram_sum, sum_sem.at[0])

    def drain(step, carry):
        up_copy(step).wait_send()

        @pl.when(step < STEPS - 1)
        def _():
            down_copy(step).wait_send()

        return carry

    lax.fori_loop(0, STEPS, drain, 0)


def on_device(user_factors, user_rows, row_counts, confidence, slot_items, prev_factors):
    conf = confidence.reshape(WINDOW, DEPTH)
    live = lax.broadcasted_iota(jnp.int32, (WINDOW, DEPTH), 1) < row_counts[:, None]
    conf = jnp.pad(jnp.where(live, conf, jnp.zeros_like(conf)), ((0, 0), (0, 8 - DEPTH)))
    vmem = pl.BlockSpec(memory_space=pltpu.VMEM)
    smem = pl.BlockSpec(memory_space=pltpu.SMEM)
    f32, bf16 = jnp.float32, jnp.bfloat16
    dma = pltpu.SemaphoreType.DMA
    return pl.pallas_call(
        kernel,
        out_shape=jax.ShapeDtypeStruct((1, 1, RANK), f32),
        in_specs=[smem, smem, vmem, vmem, vmem],
        out_specs=vmem,
        scratch_shapes=[
            pltpu.VMEM((USERS, RANK), f32),
            pltpu.VMEM((PEERS * ROWS, RANK), f32),
            pltpu.VMEM((CHUNKS, PEERS, ROWS, RANK), bf16),
            pltpu.VMEM((CHUNKS, PEERS, ROWS, RANK), bf16),
            pltpu.VMEM((PEERS * 8 * GROUP, RANK), f32),
            pltpu.VMEM((WINDOW, RANK), f32),
            pltpu.VMEM((WINDOW, RANK), f32),
            pltpu.VMEM((PEERS, 16, RANK), bf16),
            pltpu.VMEM((PEERS, 16, RANK), bf16),
            pltpu.VMEM((PLANES, PEERS * 8), f32),
            pltpu.VMEM((PLANES, PEERS * 8), f32),
            pltpu.VMEM((RANK, RANK), f32),
            pltpu.VMEM((RANK, RANK), f32),
            pltpu.VMEM((16, SLICE, RANK), f32),
            pltpu.VMEM((SLICE, RANK), f32),
            pltpu.VMEM((16, SLICE, RANK), f32),
            pltpu.VMEM((UNIT, RANK), f32),
            pltpu.VMEM((STEPS, UNIT, RANK), f32),
            pltpu.VMEM((STEPS, UNIT, RANK), f32),
            pltpu.VMEM((STEPS, UNIT, RANK), f32),
            pltpu.VMEM((STEPS, UNIT, RANK), f32),
            dma((CHUNKS,)), dma((CHUNKS,)), dma((CHUNKS,)), dma, dma, dma, dma((2,)), dma((2,)), dma((2,)),
            dma((STEPS,)), dma((STEPS,)), dma((STEPS,)), dma((STEPS,)),
        ],
        compiler_params=pltpu.CompilerParams(
            collective_id=0, has_side_effects=True, vmem_limit_bytes=48 * 1024 * 1024
        ),
    )(slot_items, user_rows, conf, user_factors, prev_factors)


def solution(mesh):
    in_specs = (
        P(("grp", "own"), None),
        P(("grp", "own")),
        P(("grp", "own")),
        P(("grp", "own")),
        P(),
        P("own", "grp", None),
    )
    out_specs = P("own", "grp", None)
    return jax.shard_map(
        on_device, mesh=mesh, in_specs=in_specs, out_specs=out_specs, check_vma=False
    )
```

time: 1020 us -> 115 us (0.11)
  waiting for transfers between devices: 852 us -> 0 us
  Pallas kernels: 0 us -> 111 us
  starting transfers between devices: 51.7 us -> 0 us
  local copies, waits for them, and re-layouts: 40.9 us -> 2.55 us
  blocking collectives: 34.6 us -> 0 us
  between operations: 21.8 us -> 0.07 us
    psum x1 -> x0, waiting for transfers between devices: 697 us -> none  [on_device(): user_gram = lax.psum(local_gram, ('grp', 'own'))]
    all_to_all x2 -> x0, waiting for transfers between devices: 155 us -> none  [the longest x1 155 us: on_device(): lax.all_to_all(outgoing, 'own', split_axis=0, concat_axis=2, tiled=True)]
    pallas_call x0 -> x1, Pallas kernels: none -> 111 us  [on_device(): pl.pallas_call(kernel, out_shape=jax.ShapeDtypeStruct((1, 1, RANK), f32),...]
    all_to_all x2 -> x0, starting transfers between devices: 51.6 us -> none  [the longest x1 29.4 us: on_device(): lax.all_to_all(conf_out, 'own', split_axis=0, concat_axis=2, tiled=True)]
    gather x7 -> x0, local copies, waits for them, and re-layouts: 36 us -> none  [the longest x2 24.5 us: on_device(): jnp.take(user_factors, picked.reshape(-1), axis=0)]
    unnamed x1 -> x0, blocking collectives: 34.6 us -> none
  transfers between devices with their start and end apart: 4 -> 0, of which waited for: 2 -> 0; matrix products, arithmetic and copies ran while one was open for 4% -> 0% of each run, Pallas kernels for 0% -> 0%
where the time goes in v1:
time: 115 us; the launch traced here: 114 us
  Pallas kernels  111 us (97%)
  local copies, waits for them, and re-layouts  2.55 us (2%)
    pallas_call x1, Pallas kernels, on_device(): pl.pallas_call(kernel, out_shape=jax.ShapeDtypeStruct((1, 1, RANK), f32),...  111 us

profile of v1, /device:TPU:6, one launch (start us, length us, event | category | flops | bytes accessed | tf_op | source)
XLA Modules:
  0.0 113.6 jit_solution(9526374381955269907)
XLA Ops:
  0.0 0.0 copy-start.4
  0.0 0.0 copy-start
  0.0 1.3 %reshape.4 = bf16[1024,6]{1,0:T(8,128)(2,1)S(1)} reshape(bf16[6144]{0:T(1024)(128)(2,1)} %param.9) | data formatting | bytes 24576 | tf_op jit(solution)/shard_map/reshape | solution.py:361
  1.3 0.0 copy-done.4
  1.3 0.2 fusion
  1.6 0.0 copy-start.1
  1.6 0.0 copy-start.2
  1.6 0.0 copy-start.3
  1.6 0.1 pad.4.conf
  1.7 0.0 copy-done
  1.7 0.6 copy-done.1
  2.3 0.0 copy-done.2
  2.3 0.0 copy-done.3
  2.3 110.7 %shard_map.64 = f32[1,1,128]{2,1,0:T(1,128)S(1)} custom-call(s32[1024]{0:T(1024)S(1)} %copy-done.2, s32[6144]{0:T(1024)S(1)} %copy-done.1, bf16[1024,8]{1,0:T(8,128)(2,1)S(1)} %pad.4.conf, bf16[4096,128]{1,0:T(8,128)(2,1)S(1)} %copy-done, f32[1,1,128]{2,1,0:T(1,128)S(1)} %copy-done.3), custom_call_target="tpu_custom_call" | custom-call | tf_op jit(solution)/shard_map/pallas_call | solution.py:368
  113.0 0.5 copy.8
Async XLA Ops:
  0.0 1.3 %copy-start.4 = (s32[1024]{0:T(1024)S(1)}, s32[1024]{0:T(1024)}, u32[]{:S(2)}) copy-start(s32[1024]{0:T(1024)} %param.8) | copy-start | bytes 12292
  0.0 1.7 %copy-start = (bf16[4096,128]{1,0:T(8,128)(2,1)S(1)}, bf16[4096,128]{1,0:T(8,128)(2,1)}, u32[]{:S(2)}) copy-start(bf16[4096,128]{1,0:T(8,128)(2,1)} %users.1) | copy-start | bytes 3145732
  1.6 0.7 copy-start.1
  1.6 0.7 copy-start.2
  1.6 0.7 copy-start.3

commit v2 on v1

v2 whole, which is shorter than its diff:
```python
import jax
import jax.numpy as jnp
from jax import lax
from jax.experimental import pallas as pl
from jax.experimental.pallas import tpu as pltpu
from jax.sharding import PartitionSpec as P

CG_STEPS = 3
RIDGE = 4.0
EPSILON = 1e-06

RANK = 128
DEPTH = 6
USERS = 4096
WINDOW = 1024
SIDE = 4
PLANES = 32
PLANE = 32
PEERS = 2 * PLANE
ITEMS = WINDOW // PEERS
CHUNKS = 2
GROUP = ITEMS // CHUNKS
STEPS = ITEMS // 2
ROWS = GROUP * DEPTH
PADDED = 8
LENGTH = PEERS * PADDED
UNIT = RANK + 8
CUTS = ((0, 32), (32, 32), (64, 32), (96, 40))
PIECE = RANK // PLANE
MESH = pl.DeviceIdType.MESH


def place():
    grp = lax.axis_index("grp")
    own = lax.axis_index("own")
    return grp // SIDE, grp % SIDE, own // 2, own % 2


def other_plane(z, core):
    odd = z % 2
    away = 1 - 2 * odd
    return (z + away * (1 - 2 * core) + PLANES) % PLANES


def peer(step):
    gx, gy, _, core = place()
    px = (gx + (step // 2) % SIDE) % SIDE
    py = (gy + step // (2 * SIDE)) % SIDE
    pc = (core + step % 2) % 2
    grp = px * SIDE + py
    return grp, pc, pc * 16 + grp


def along(step):
    _, _, z, core = place()
    return (lax.axis_index("grp"), ((z + step + PLANES) % PLANES) * 2 + core)


def solve(system, rhs, start):
    row = lax.broadcasted_iota(jnp.int32, (RANK, RANK), 0)
    col = lax.broadcasted_iota(jnp.int32, (RANK, RANK), 1)
    same = row == col

    def applied_to(vector):
        column = jnp.sum(system * vector, axis=1, keepdims=True)
        return jnp.sum(jnp.where(same, column, 0.0), axis=0, keepdims=True)

    answer = start
    residual = rhs - applied_to(start)
    direction = residual
    norm_now = jnp.sum(residual * residual, axis=1, keepdims=True)
    for step in range(CG_STEPS):
        applied = applied_to(direction)
        step_size = norm_now / (jnp.sum(direction * applied, axis=1, keepdims=True) + EPSILON)
        answer = answer + step_size * direction
        residual = residual - step_size * applied
        norm_next = jnp.sum(residual * residual, axis=1, keepdims=True)
        direction = residual + (norm_next / (norm_now + EPSILON)) * direction
        norm_now = norm_next
    return answer


def kernel(
    items, rows, conf, users, start, out,
    wide, stage, send, recv, flat, conf_wide, conf_stage, conf_send, conf_recv, conf_all, weight_all,
    gram_own, gram_cut, gram_parts, gram_piece, gram_planes, gram_total, gram_all,
    up_send, up_recv, down_send, down_recv,
    send_sem, recv_sem, self_sem, conf_send_sem, conf_recv_sem, conf_self_sem, part_sem, plane_sem, all_sem,
    up_send_sem, up_recv_sem, down_send_sem, down_recv_sem,
):
    _, _, z, core = place()
    me = core * 16 + lax.axis_index("grp")
    barrier = pltpu.get_barrier_semaphore()

    def greet(device):
        pl.semaphore_signal(barrier, inc=1, device_id=device, device_id_type=MESH)

    def greet_plane(step, carry):
        grp, pc, _ = peer(step)

        @pl.when(step > 0)
        def _():
            greet((grp, z * 2 + pc))
            greet(along(step))

        greet((grp, other_plane(z, core) * 2 + pc))
        return carry

    lax.fori_loop(0, PLANE, greet_plane, 0)

    def widen_users(block, carry):
        at = pl.ds(pl.multiple_of(block * 512, 512), 512)
        wide[at, :] = users[at, :].astype(jnp.float32)
        return carry

    lax.fori_loop(0, USERS // 512, widen_users, 0)

    def gather(chunk):
        def owner(to, carry):
            d = to % PLANE
            far = other_plane(z, d // 16)
            base = jnp.where(to < PLANE, z, far)
            for index in range(GROUP):
                step = chunk * (GROUP // 2) + index // 2
                away = STEPS - step if index % 2 == 0 else step - (STEPS - 1)
                item = items[((base + 2 * away + PLANES) % PLANES) * PLANE + d]
                for slot in range(DEPTH):
                    row = rows[item * DEPTH + slot]
                    stage[pl.ds(to * ROWS + slot * GROUP + index, 1), :] = wide[pl.ds(row, 1), :]
            return carry

        lax.fori_loop(0, PEERS, owner, 0)

        def narrow(block, carry):
            at = pl.ds(pl.multiple_of(block * ROWS * 4, ROWS * 4), ROWS * 4)
            part = stage[at, :].astype(jnp.bfloat16)
            send[chunk, pl.ds(block * 4, 4)] = part.reshape(4, ROWS, RANK)
            return carry

        lax.fori_loop(0, PEERS // 4, narrow, 0)

    def post(source, target, send_to, recv_from, self_to):
        def one(step, carry):
            grp, pc, d = peer(step)

            @pl.when(step > 0)
            def _():
                pltpu.make_async_remote_copy(
                    src_ref=source(d), dst_ref=target(me), send_sem=send_to, recv_sem=recv_from,
                    device_id=(grp, z * 2 + pc), device_id_type=MESH,
                ).start()

            pltpu.make_async_remote_copy(
                src_ref=source(PLANE + d), dst_ref=target(PLANE + me), send_sem=send_to, recv_sem=recv_from,
                device_id=(grp, other_plane(z, pc) * 2 + pc), device_id_type=MESH,
            ).start()
            return carry

        lax.fori_loop(0, PLANE, one, 0)
        pltpu.make_async_copy(source(me), target(me), self_to).start()

    def wait_blocks(ref, count, sem):
        pltpu.make_async_copy(ref.at[pl.ds(0, count)], ref.at[pl.ds(0, count)], sem).wait()

    def post_rows(chunk):
        post(
            lambda d: send.at[chunk, d], lambda d: recv.at[chunk, d],
            send_sem.at[chunk], recv_sem.at[chunk], self_sem.at[chunk],
        )

    def post_conf():
        spread_row = lax.broadcasted_iota(jnp.int32, (8, RANK), 0)
        spread_col = lax.broadcasted_iota(jnp.int32, (8, RANK), 1)
        mine = spread_col // PADDED == me % 16
        spread = jnp.where(jnp.logical_and(mine, spread_col % PADDED == spread_row), 1.0, 0.0).astype(jnp.bfloat16)
        conf_wide[...] = jnp.dot(conf[...], spread, preferred_element_type=jnp.float32)

        def owner(to, carry):
            d = to % PLANE
            far = other_plane(z, d // 16)
            base = jnp.where(to < PLANE, z, far)
            for index in range(ITEMS):
                step = index // 2
                away = STEPS - step if index % 2 == 0 else step - (STEPS - 1)
                item = items[((base + 2 * away + PLANES) % PLANES) * PLANE + d]
                conf_stage[pl.ds(to * ITEMS + index, 1), :] = conf_wide[pl.ds(item, 1), :]
            return carry

        lax.fori_loop(0, PEERS, owner, 0)

        def narrow(block, carry):
            at = pl.ds(pl.multiple_of(block * ITEMS * 8, ITEMS * 8), ITEMS * 8)
            conf_send[pl.ds(block * 8, 8)] = conf_stage[at, :].astype(jnp.bfloat16).reshape(8, ITEMS, RANK)
            return carry

        lax.fori_loop(0, PEERS // 8, narrow, 0)
        post(lambda d: conf_send.at[d], lambda d: conf_recv.at[d], conf_send_sem, conf_recv_sem, conf_self_sem)

    def take_conf():
        wait_blocks(conf_recv, PEERS - 1, conf_recv_sem)
        pltpu.make_async_copy(conf_send.at[me], conf_recv.at[me], conf_self_sem).wait()
        for part in range(PEERS // 16):
            total = jnp.zeros((ITEMS, RANK), jnp.float32)
            for index in range(16):
                total = total + conf_recv[part * 16 + index].astype(jnp.float32)
            conf_all[:, pl.ds(part * RANK, RANK)] = total
        values = conf_all[...]
        weight = (1.0 + values).astype(jnp.bfloat16).astype(jnp.float32)
        weight_all[...] = jnp.where(values > 0.0, weight, 0.0)

    def post_gram():
        gram_own[...] = jnp.zeros_like(gram_own)

        def one_block(block, carry):
            part = users[pl.ds(pl.multiple_of(block * 512, 512), 512), :]
            gram_own[...] += lax.dot_general(part, part, (((0,), (0,)), ((), ())), preferred_element_type=jnp.float32)
            return carry

        lax.fori_loop(0, USERS // 512, one_block, 0)
        for index in range(PLANE):
            gram_cut[index] = gram_own[pl.ds(index * PIECE, PIECE), :]

        def one(step, carry):
            grp, pc, d = peer(step)
            pltpu.make_async_remote_copy(
                src_ref=gram_cut.at[d], dst_ref=gram_parts.at[me], send_sem=part_sem.at[0],
                recv_sem=part_sem.at[1], device_id=(grp, z * 2 + pc), device_id_type=MESH,
            ).start()
            return carry

        lax.fori_loop(1, PLANE, one, 0)
        gram_parts[me] = gram_cut[me]

    def post_piece():
        wait_blocks(gram_parts, PLANE - 1, part_sem.at[1])
        total = jnp.sum(gram_parts[...], axis=0)
        gram_piece[...] = total

        def one(step, carry):
            pltpu.make_async_remote_copy(
                src_ref=gram_piece, dst_ref=gram_planes.at[z], send_sem=plane_sem.at[0],
                recv_sem=plane_sem.at[1], device_id=along(step), device_id_type=MESH,
            ).start()
            return carry

        lax.fori_loop(1, PLANES, one, 0)
        gram_planes[z] = total

    def post_total():
        wait_blocks(gram_planes, PLANES - 1, plane_sem.at[1])
        total = jnp.sum(gram_planes[...], axis=0)
        gram_total[...] = total

        def one(step, carry):
            grp, pc, d = peer(step)
            pltpu.make_async_remote_copy(
                src_ref=gram_total, dst_ref=gram_all.at[me], send_sem=all_sem.at[0],
                recv_sem=all_sem.at[1], device_id=(grp, z * 2 + pc), device_id_type=MESH,
            ).start()
            return carry

        lax.fori_loop(1, PLANE, one, 0)
        gram_all[me] = total

    def item_gram(into, at, index):
        values = flat[pl.ds(index, LENGTH, stride=GROUP), :]
        scaled = (jnp.transpose(values) * conf_all[pl.ds(at, 1), :]).astype(jnp.bfloat16)
        weights = jnp.broadcast_to(weight_all[pl.ds(at, 1), :], (16, LENGTH)).astype(jnp.bfloat16)
        left = jnp.concatenate([scaled, weights], axis=0)
        product = jnp.dot(left, values.astype(jnp.bfloat16), preferred_element_type=jnp.float32)
        into[...] = product[:UNIT]

    def up_copy(step, part):
        first, count = CUTS[part]
        at = pl.ds(first, count)
        return pltpu.make_async_remote_copy(
            src_ref=up_send.at[step, at], dst_ref=up_recv.at[step, at], send_sem=up_send_sem.at[step, part],
            recv_sem=up_recv_sem.at[step, part], device_id=along(2), device_id_type=MESH,
        )

    def down_copy(step, part):
        first, count = CUTS[part]
        at = pl.ds(first, count)
        return pltpu.make_async_remote_copy(
            src_ref=down_send.at[step, at], dst_ref=down_recv.at[step, at], send_sem=down_send_sem.at[step, part],
            recv_sem=down_recv_sem.at[step, part], device_id=along(-2), device_id_type=MESH,
        )

    for index in range(LENGTH * GROUP // 256):
        flat[pl.ds(index * 256, 256), :] = jnp.zeros((256, RANK), jnp.float32)
    gather(0)
    pl.semaphore_wait(barrier, 2 * (PLANE - 1) + PLANE)
    post_rows(0)
    post_conf()
    post_gram()
    gather(1)
    post_rows(1)
    take_conf()

    def chain(step, carry):
        chunk = step // (GROUP // 2)
        index = (step % (GROUP // 2)) * 2

        @pl.when(index == 0)
        def _():
            pltpu.make_async_copy(
                recv.at[chunk, pl.ds(0, PEERS - 1)], recv.at[chunk, pl.ds(0, PEERS - 1)], recv_sem.at[chunk]
            ).wait()
            pltpu.make_async_copy(send.at[chunk, me], recv.at[chunk, me], self_sem.at[chunk]).wait()

            def widen(source, carry):
                at = pl.ds(pl.multiple_of(source * PADDED * GROUP, PADDED * GROUP), ROWS)
                flat[at, :] = recv[chunk, source].astype(jnp.float32)
                return carry

            lax.fori_loop(0, PEERS, widen, 0)

        item_gram(up_send.at[step], step * 2, index)
        item_gram(down_send.at[step], step * 2 + 1, index + 1)

        for part, (first, count) in enumerate(CUTS):
            at = pl.ds(first, count)

            @pl.when(step > 0)
            def _():
                up_copy(step - 1, part).wait_recv()
                up_send[step, at] += up_recv[step - 1, at]

            up_copy(step, part).start()

            @pl.when(step > 0)
            def _():
                down_copy(step - 1, part).wait_recv()
                down_send[step, at] += down_recv[step - 1, at]

            @pl.when(step < STEPS - 1)
            def _():
                down_copy(step, part).start()

        @pl.when(step == 1)
        def _():
            post_piece()

        @pl.when(step == 4)
        def _():
            post_total()

        return carry

    lax.fori_loop(0, STEPS, chain, 0)
    wait_blocks(gram_all, PLANE - 1, all_sem.at[1])
    row = lax.broadcasted_iota(jnp.int32, (RANK, RANK), 0)
    col = lax.broadcasted_iota(jnp.int32, (RANK, RANK), 1)
    for index in range(PLANE):
        gram_own[pl.ds(index * PIECE, PIECE), :] = gram_all[index]
    gram_own[...] += jnp.where(row == col, RIDGE, 0.0) + down_send[STEPS - 1, pl.ds(0, RANK)]
    for part in range(len(CUTS)):
        up_copy(STEPS - 1, part).wait_recv()
    system = gram_own[...] + up_recv[STEPS - 1, pl.ds(0, RANK)]
    rhs = down_send[STEPS - 1, pl.ds(RANK, 1)] + up_recv[STEPS - 1, pl.ds(RANK, 1)]
    out[0] = solve(system, rhs, start[0])

    for chunk in range(CHUNKS):
        pltpu.make_async_copy(
            send.at[chunk, pl.ds(0, PEERS - 1)], send.at[chunk, pl.ds(0, PEERS - 1)], send_sem.at[chunk]
        ).wait()
    wait_blocks(conf_send, PEERS - 1, conf_send_sem)
    wait_blocks(gram_parts, PLANE - 1, part_sem.at[0])
    wait_blocks(gram_planes, PLANES - 1, plane_sem.at[0])
    wait_blocks(gram_all, PLANE - 1, all_sem.at[0])

    def drain(step, carry):
        for part in range(len(CUTS)):
            up_copy(step, part).wait_send()

            @pl.when(step < STEPS - 1)
            def _():
                down_copy(step, part).wait_send()

        return carry

    lax.fori_loop(0, STEPS, drain, 0)


def on_device(user_factors, user_rows, row_counts, confidence, slot_items, prev_factors):
    conf = confidence.reshape(WINDOW, DEPTH)
    live = lax.broadcasted_iota(jnp.int32, (WINDOW, DEPTH), 1) < row_counts[:, None]
    conf = jnp.pad(jnp.where(live, conf, jnp.zeros_like(conf)), ((0, 0), (0, 8 - DEPTH)))
    vmem = pl.BlockSpec(memory_space=pltpu.VMEM)
    smem = pl.BlockSpec(memory_space=pltpu.SMEM)
    f32, bf16 = jnp.float32, jnp.bfloat16
    dma = pltpu.SemaphoreType.DMA
    parts = len(CUTS)
    return pl.pallas_call(
        kernel,
        out_shape=jax.ShapeDtypeStruct((1, 1, RANK), f32),
        in_specs=[smem, smem, vmem, vmem, vmem],
        out_specs=vmem,
        scratch_shapes=[
            pltpu.VMEM((USERS, RANK), f32),
            pltpu.VMEM((PEERS * ROWS, RANK), f32),
            pltpu.VMEM((CHUNKS, PEERS, ROWS, RANK), bf16),
            pltpu.VMEM((CHUNKS, PEERS, ROWS, RANK), bf16),
            pltpu.VMEM((LENGTH * GROUP, RANK), f32),
            pltpu.VMEM((WINDOW, RANK), f32),
            pltpu.VMEM((WINDOW, RANK), f32),
            pltpu.VMEM((PEERS, ITEMS, RANK), bf16),
            pltpu.VMEM((PEERS, ITEMS, RANK), bf16),
            pltpu.VMEM((ITEMS, LENGTH), f32),
            pltpu.VMEM((ITEMS, LENGTH), f32),
            pltpu.VMEM((RANK, RANK), f32),
            pltpu.VMEM((PLANE, PIECE, RANK), f32),
            pltpu.VMEM((PLANE, PIECE, RANK), f32),
            pltpu.VMEM((PIECE, RANK), f32),
            pltpu.VMEM((PLANES, PIECE, RANK), f32),
            pltpu.VMEM((PIECE, RANK), f32),
            pltpu.VMEM((PLANE, PIECE, RANK), f32),
            pltpu.VMEM((STEPS, UNIT, RANK), f32),
            pltpu.VMEM((STEPS, UNIT, RANK), f32),
            pltpu.VMEM((STEPS, UNIT, RANK), f32),
            pltpu.VMEM((STEPS, UNIT, RANK), f32),
            dma((CHUNKS,)), dma((CHUNKS,)), dma((CHUNKS,)), dma, dma, dma, dma((2,)), dma((2,)), dma((2,)),
            dma((STEPS, parts)), dma((STEPS, parts)), dma((STEPS, parts)), dma((STEPS, parts)),
        ],
        compiler_params=pltpu.CompilerParams(
            collective_id=0, has_side_effects=True, vmem_limit_bytes=48 * 1024 * 1024
        ),
    )(slot_items, user_rows, conf, user_factors, prev_factors)


def solution(mesh):
    in_specs = (
        P(("grp", "own"), None),
        P(("grp", "own")),
        P(("grp", "own")),
        P(("grp", "own")),
        P(),
        P("own", "grp", None),
    )
    out_specs = P("own", "grp", None)
    return jax.shard_map(
        on_device, mesh=mesh, in_specs=in_specs, out_specs=out_specs, check_vma=False
    )
```

time: 115 us -> 93.6 us (0.81); the launches traced: 114 us -> 93.4 us
  Pallas kernels: 111 us -> 90.5 us
    pallas_call x1, Pallas kernels: 111 us -> 90.5 us  [on_device(): pl.pallas_call(kernel, out_shape=jax.ShapeDtypeStruct((1, 1, RANK), f32),...]
where the time goes in v2:
time: 93.6 us; the launch traced here: 93.4 us
  Pallas kernels  90.5 us (97%)
  local copies, waits for them, and re-layouts  2.55 us (3%)
    pallas_call x1, Pallas kernels, on_device(): pl.pallas_call(kernel, out_shape=jax.ShapeDtypeStruct((1, 1, RANK), f32),...  90.5 us

profile of v2, /device:TPU:6, one launch (start us, length us, event | category | flops | bytes accessed | tf_op | source)
XLA Modules:
  0.0 93.4 jit_solution(7333856591031964471)
XLA Ops:
  0.0 0.0 copy-start.4
  0.0 0.0 copy-start
  0.0 1.3 %reshape.4 = bf16[1024,6]{1,0:T(8,128)(2,1)S(1)} reshape(bf16[6144]{0:T(1024)(128)(2,1)} %param.9) | data formatting | bytes 24576 | tf_op jit(solution)/shard_map/reshape | solution.py:386
  1.3 0.0 copy-done.4
  1.3 0.2 fusion
  1.6 0.0 copy-start.1
  1.6 0.0 copy-start.2
  1.6 0.0 copy-start.3
  1.6 0.1 pad.4.conf
  1.7 0.0 copy-done
  1.7 0.6 copy-done.1
  2.3 0.0 copy-done.2
  2.3 0.0 copy-done.3
  2.3 90.5 %shard_map.64 = f32[1,1,128]{2,1,0:T(1,128)S(1)} custom-call(s32[1024]{0:T(1024)S(1)} %copy-done.2, s32[6144]{0:T(1024)S(1)} %copy-done.1, bf16[1024,8]{1,0:T(8,128)(2,1)S(1)} %pad.4.conf, bf16[4096,128]{1,0:T(8,128)(2,1)S(1)} %copy-done, f32[1,1,128]{2,1,0:T(1,128)S(1)} %copy-done.3), custom_call_target="tpu_custom_call" | custom-call | tf_op jit(solution)/shard_map/pallas_call | solution.py:394
  92.8 0.5 copy.8
Async XLA Ops:
  0.0 1.3 %copy-start.4 = (s32[1024]{0:T(1024)S(1)}, s32[1024]{0:T(1024)}, u32[]{:S(2)}) copy-start(s32[1024]{0:T(1024)} %param.8) | copy-start | bytes 12292
  0.0 1.7 %copy-start = (bf16[4096,128]{1,0:T(8,128)(2,1)S(1)}, bf16[4096,128]{1,0:T(8,128)(2,1)}, u32[]{:S(2)}) copy-start(bf16[4096,128]{1,0:T(8,128)(2,1)} %users.1) | copy-start | bytes 3145732
  1.6 0.7 copy-start.1
  1.6 0.7 copy-start.2
  1.6 0.7 copy-start.3

commit v3 on v2

v3 whole, which is shorter than its diff:
```python
import jax
import jax.numpy as jnp
from jax import lax
from jax.experimental import pallas as pl
from jax.experimental.pallas import tpu as pltpu
from jax.sharding import PartitionSpec as P

CG_STEPS = 3
RIDGE = 4.0
EPSILON = 1e-06

RANK = 128
DEPTH = 6
USERS = 4096
WINDOW = 1024
SIDE = 4
PLANES = 32
PLANE = 32
PEERS = 2 * PLANE
ITEMS = WINDOW // PEERS
STEPS = ITEMS // 2
PADDED = 8
LENGTH = PEERS * PADDED
CHUNKS = ((0, 1), (1, 3), (4, 4))
SIZES = tuple(2 * steps * PADDED for _, steps in CHUNKS)
UNIT = RANK + 8
CUTS = ((0, 64), (64, 72))
PIECE = RANK // PLANE
MESH = pl.DeviceIdType.MESH


def place():
    grp = lax.axis_index("grp")
    own = lax.axis_index("own")
    return grp // SIDE, grp % SIDE, own // 2, own % 2


def wrapped(number, size):
    number = jnp.where(number < 0, number + size, number)
    return jnp.where(number >= size, number - size, number)


def other_plane(z, core):
    away = 1 - 2 * (z % 2)
    return wrapped(z + away * (1 - 2 * core), PLANES)


def along(step):
    _, _, z, core = place()
    return (lax.axis_index("grp"), wrapped(z + step, PLANES) * 2 + core)


def each_peer(act):
    gx, gy, _, core = place()
    cores = (core, 1 - core)
    columns = [wrapped(gy + step, SIDE) for step in range(SIDE)]

    def ring(step, line):
        for dy in (2, 3, 1, 0):
            for dc in range(2):
                grp = line * SIDE + columns[dy]
                act(grp, cores[dc], cores[dc] * 16 + grp, step == 2 if dy + dc == 0 else None)
        return wrapped(line + 1, SIDE)

    lax.fori_loop(0, SIDE, ring, wrapped(gx + 2, SIDE))


def unless(first, act):
    if first is None:
        act()
    else:
        pl.when(jnp.logical_not(first))(act)


def solve(system, rhs, start):
    row = lax.broadcasted_iota(jnp.int32, (RANK, RANK), 0)
    col = lax.broadcasted_iota(jnp.int32, (RANK, RANK), 1)
    same = row == col

    def applied_to(vector):
        column = jnp.sum(system * vector, axis=1, keepdims=True)
        return jnp.sum(jnp.where(same, column, 0.0), axis=0, keepdims=True)

    answer = start
    residual = rhs - applied_to(start)
    direction = residual
    norm_now = jnp.sum(residual * residual, axis=1, keepdims=True)
    for step in range(CG_STEPS):
        applied = applied_to(direction)
        step_size = norm_now / (jnp.sum(direction * applied, axis=1, keepdims=True) + EPSILON)
        answer = answer + step_size * direction
        residual = residual - step_size * applied
        norm_next = jnp.sum(residual * residual, axis=1, keepdims=True)
        direction = residual + (norm_next / (norm_now + EPSILON)) * direction
        norm_now = norm_next
    return answer


def kernel(
    items, rows, conf, users, start, out,
    wide, stage, send, recv, flat, conf_wide, conf_parts, conf_all, weight_all,
    gram_own, gram_cut, gram_parts, gram_piece, gram_all, piece_send, piece_recv,
    up_send, up_recv, down_send, down_recv,
    send_sem, recv_sem, self_sem, part_sem, all_sem, piece_send_sem, piece_recv_sem,
    up_send_sem, up_recv_sem, down_send_sem, down_recv_sem,
):
    _, _, z, core = place()
    me = core * 16 + lax.axis_index("grp")
    barrier = pltpu.get_barrier_semaphore()

    def greet(device):
        pl.semaphore_signal(barrier, inc=1, device_id=device, device_id_type=MESH)

    far_plane = other_plane(z, core)
    far_planes = (other_plane(z, 0), other_plane(z, 1))

    def greet_plane(grp, pc, _, first):
        unless(first, lambda: greet((grp, z * 2 + pc)))
        greet((grp, far_plane * 2 + pc))

    each_peer(greet_plane)
    for away in (2, -2, 4, -4):
        greet(along(away))

    def widen_users(block, carry):
        at = pl.ds(pl.multiple_of(block * 512, 512), 512)
        wide[at, :] = users[at, :].astype(jnp.float32)
        return carry

    lax.fori_loop(0, USERS // 512, widen_users, 0)

    def item_of(base, d, index):
        step = index // 2
        away = STEPS - step if index % 2 == 0 else step - (STEPS - 1)
        return items[wrapped(base + 2 * away, PLANES) * PLANE + d]

    def each_receiver(act):
        for far in range(2):
            for pc in range(2):
                base = far_planes[pc] if far else z

                def one(grp, carry):
                    act(far * PLANE + pc * 16 + grp, pc * 16 + grp, base)
                    return carry

                lax.fori_loop(0, 16, one, 0)

    def spread_conf():
        spread_row = lax.broadcasted_iota(jnp.int32, (8, RANK), 0)
        spread_col = lax.broadcasted_iota(jnp.int32, (8, RANK), 1)
        mine = spread_col // PADDED == me % 16
        spread = jnp.where(jnp.logical_and(mine, spread_col % PADDED == spread_row), 1.0, 0.0).astype(jnp.bfloat16)
        conf_wide[...] = jnp.dot(conf[...], spread, preferred_element_type=jnp.float32)

    def gather(chunk):
        first, count = CHUNKS[chunk]
        group, size = 2 * count, SIZES[chunk]

        def owner(to, d, base):
            for index in range(group):
                item = item_of(base, d, 2 * first + index)
                for slot in range(DEPTH):
                    row = rows[item * DEPTH + slot]
                    stage[pl.ds(to * size + slot * group + index, 1), :] = wide[pl.ds(row, 1), :]
                stage[pl.ds(to * size + DEPTH * group + index, 1), :] = conf_wide[pl.ds(item, 1), :]

        each_receiver(owner)

        def narrow(block, carry):
            at = pl.ds(pl.multiple_of(block * size * 4, size * 4), size * 4)
            part = stage[at, :].astype(jnp.bfloat16)
            send[chunk, pl.ds(block * 4, 4), pl.ds(0, size)] = part.reshape(4, size, RANK)
            return carry

        lax.fori_loop(0, PEERS // 4, narrow, 0)

    def post_rows(chunk):
        size = pl.ds(0, SIZES[chunk])

        def one(grp, pc, d, first):
            def near():
                pltpu.make_async_remote_copy(
                    src_ref=send.at[chunk, d, size], dst_ref=recv.at[chunk, me, size], send_sem=send_sem.at[chunk],
                    recv_sem=recv_sem.at[chunk], device_id=(grp, z * 2 + pc), device_id_type=MESH,
                ).start()

            unless(first, near)
            far = jnp.where(pc == 0, far_planes[0], far_planes[1])
            pltpu.make_async_remote_copy(
                src_ref=send.at[chunk, PLANE + d, size], dst_ref=recv.at[chunk, PLANE + me, size],
                send_sem=send_sem.at[chunk], recv_sem=recv_sem.at[chunk], device_id=(grp, far * 2 + pc),
                device_id_type=MESH,
            ).start()

        each_peer(one)
        own_rows(chunk).start()

    def own_rows(chunk):
        size = pl.ds(0, SIZES[chunk])
        return pltpu.make_async_copy(send.at[chunk, me, size], recv.at[chunk, me, size], self_sem.at[chunk])

    def wait_rows(ref, chunk, sem):
        part = ref.at[chunk, pl.ds(0, PEERS - 1), pl.ds(0, SIZES[chunk])]
        pltpu.make_async_copy(part, part, sem.at[chunk]).wait()

    def wait_blocks(ref, count, sem):
        pltpu.make_async_copy(ref.at[pl.ds(0, count)], ref.at[pl.ds(0, count)], sem).wait()

    def take_rows(chunk):
        wait_rows(recv, chunk, recv_sem)
        own_rows(chunk).wait()
        group, size = 2 * CHUNKS[chunk][1], SIZES[chunk]
        used = DEPTH * group
        tail = used // 8 * 8
        live = lax.broadcasted_iota(jnp.int32, (size, RANK), 0) < used

        def sixteen(part, carry):
            def widen(index, total):
                source = part * 16 + index
                block = recv[chunk, source, pl.ds(0, size)].astype(jnp.float32)
                flat[pl.ds(pl.multiple_of(source * size, size), size), :] = jnp.where(live, block, 0.0)
                return total + block[tail:]

            total = lax.fori_loop(0, 16, widen, jnp.zeros((size - tail, RANK), jnp.float32))
            conf_parts[part, pl.ds(0, size - tail)] = total
            return carry

        lax.fori_loop(0, PEERS // 16, sixteen, 0)
        for part in range(PEERS // 16):
            at = pl.ds(part * RANK, RANK)
            conf_all[chunk, pl.ds(0, group), at] = conf_parts[part, pl.ds(used - tail, group)]
        values = conf_all[chunk]
        weight = (1.0 + values).astype(jnp.bfloat16).astype(jnp.float32)
        weight_all[chunk] = jnp.where(values > 0.0, weight, 0.0)

    def own_gram():
        gram_own[...] = jnp.zeros_like(gram_own)

        def one_block(block, carry):
            part = users[pl.ds(pl.multiple_of(block * 512, 512), 512), :]
            gram_own[...] += lax.dot_general(part, part, (((0,), (0,)), ((), ())), preferred_element_type=jnp.float32)
            return carry

        lax.fori_loop(0, USERS // 512, one_block, 0)
        for index in range(PLANE):
            gram_cut[index] = gram_own[pl.ds(index * PIECE, PIECE), :]

    def post_gram():
        def one(grp, pc, d, first):
            def start_copy():
                pltpu.make_async_remote_copy(
                    src_ref=gram_cut.at[d], dst_ref=gram_parts.at[me], send_sem=part_sem.at[0],
                    recv_sem=part_sem.at[1], device_id=(grp, z * 2 + pc), device_id_type=MESH,
                ).start()

            unless(first, start_copy)

        each_peer(one)
        gram_parts[me] = gram_cut[me]

    def pair_copy():
        return pltpu.make_async_remote_copy(
            src_ref=piece_send.at[0], dst_ref=piece_recv.at[0], send_sem=piece_send_sem.at[0],
            recv_sem=piece_recv_sem.at[0], device_id=(lax.axis_index("grp"), far_plane * 2 + core), device_id_type=MESH,
        )

    def next_copy():
        return pltpu.make_async_remote_copy(
            src_ref=piece_send.at[1], dst_ref=piece_recv.at[1], send_sem=piece_send_sem.at[1],
            recv_sem=piece_recv_sem.at[1], device_id=along(2), device_id_type=MESH,
        )

    def round_copy(turn, down):
        at = 2 + 4 * down + turn
        return pltpu.make_async_remote_copy(
            src_ref=piece_send.at[2] if turn == 0 else piece_recv.at[at - 1], dst_ref=piece_recv.at[at],
            send_sem=piece_send_sem.at[at], recv_sem=piece_recv_sem.at[at], device_id=along(-4 if down else 4),
            device_id_type=MESH,
        )

    def pair_turn():
        wait_blocks(gram_parts, PLANE - 1, part_sem.at[1])
        piece_send[0] = jnp.sum(gram_parts[...], axis=0)
        pair_copy().start()

    def next_turn():
        pair_copy().wait_recv()
        piece_send[1] = piece_send[0] + piece_recv[0]
        next_copy().start()

    def round_turn(turn):
        if turn == 0:
            next_copy().wait_recv()
            piece_send[2] = piece_send[1] + piece_recv[1]
        else:
            round_copy(turn - 1, 0).wait_recv()
            if turn < 4:
                round_copy(turn - 1, 1).wait_recv()
        if turn < 4:
            round_copy(turn, 0).start()
        if turn < 3:
            round_copy(turn, 1).start()

    def post_total():
        total = jnp.sum(piece_recv[pl.ds(2, 7)], axis=0) + piece_send[2]
        gram_piece[...] = total

        def one(grp, pc, d, first):
            def start_copy():
                pltpu.make_async_remote_copy(
                    src_ref=gram_piece, dst_ref=gram_all.at[me], send_sem=all_sem.at[0],
                    recv_sem=all_sem.at[1], device_id=(grp, z * 2 + pc), device_id_type=MESH,
                ).start()

            unless(first, start_copy)

        each_peer(one)
        gram_all[me] = total

    def beside(step):
        if step == 0:
            next_turn()
        elif step < 6:
            round_turn(step - 1)
        if step == 5:
            post_total()

    def item_gram(into, chunk, index):
        values = flat[pl.ds(index, LENGTH, stride=2 * CHUNKS[chunk][1]), :]
        scaled = (jnp.transpose(values) * conf_all[chunk, pl.ds(index, 1), :]).astype(jnp.bfloat16)
        weights = jnp.broadcast_to(weight_all[chunk, pl.ds(index, 1), :], (16, LENGTH)).astype(jnp.bfloat16)
        left = jnp.concatenate([scaled, weights], axis=0)
        product = jnp.dot(left, values.astype(jnp.bfloat16), preferred_element_type=jnp.float32)
        into[...] = product[:UNIT]

    def up_copy(step, part):
        first, count = CUTS[part]
        at = pl.ds(first, count)
        return pltpu.make_async_remote_copy(
            src_ref=up_send.at[step, at], dst_ref=up_recv.at[step, at], send_sem=up_send_sem.at[step, part],
            recv_sem=up_recv_sem.at[step, part], device_id=along(2), device_id_type=MESH,
        )

    def down_copy(step, part):
        first, count = CUTS[part]
        at = pl.ds(first, count)
        return pltpu.make_async_remote_copy(
            src_ref=down_send.at[step, at], dst_ref=down_recv.at[step, at], send_sem=down_send_sem.at[step, part],
            recv_sem=down_recv_sem.at[step, part], device_id=along(-2), device_id_type=MESH,
        )

    stage[...] = jnp.zeros_like(stage)
    spread_conf()
    gather(0)
    pl.semaphore_wait(barrier, PLANE - 1 + PLANE + 4)
    post_rows(0)
    own_gram()
    post_gram()
    gather(1)
    post_rows(1)
    gather(2)
    post_rows(2)

    def chain(step, chunk):
        index = (step - CHUNKS[chunk][0]) * 2
        item_gram(up_send.at[step], chunk, index)
        item_gram(down_send.at[step], chunk, index + 1)
        for part, (begin, count) in enumerate(CUTS):
            at = pl.ds(begin, count)
            if step > 0:
                up_copy(step - 1, part).wait_recv()
                up_send[step, at] += up_recv[step - 1, at]
            up_copy(step, part).start()
            if step > 0:
                down_copy(step - 1, part).wait_recv()
                down_send[step, at] += down_recv[step - 1, at]
            if step < STEPS - 1:
                down_copy(step, part).start()
        beside(step)

    for chunk, (first, count) in enumerate(CHUNKS):
        if chunk == 0:
            pair_turn()
        take_rows(chunk)
        for step in range(first, first + count):
            chain(step, chunk)
    row = lax.broadcasted_iota(jnp.int32, (RANK, RANK), 0)
    col = lax.broadcasted_iota(jnp.int32, (RANK, RANK), 1)
    wait_blocks(gram_all, PLANE - 1, all_sem.at[1])
    for index in range(PLANE):
        gram_own[pl.ds(index * PIECE, PIECE), :] = gram_all[index]
    gram_own[...] += down_send[STEPS - 1, pl.ds(0, RANK)] + jnp.where(row == col, RIDGE, 0.0)
    for part in range(len(CUTS)):
        up_copy(STEPS - 1, part).wait_recv()
    system = gram_own[...] + up_recv[STEPS - 1, pl.ds(0, RANK)]
    rhs = down_send[STEPS - 1, pl.ds(RANK, 1)] + up_recv[STEPS - 1, pl.ds(RANK, 1)]
    out[0] = solve(system, rhs, start[0])

    for chunk in range(len(CHUNKS)):
        wait_rows(send, chunk, send_sem)
    wait_blocks(gram_parts, PLANE - 1, part_sem.at[0])
    pair_copy().wait_send()
    next_copy().wait_send()
    for turn in range(4):
        round_copy(turn, 0).wait_send()
    for turn in range(3):
        round_copy(turn, 1).wait_send()
    wait_blocks(gram_all, PLANE - 1, all_sem.at[0])

    def drain(step, carry):
        for part in range(len(CUTS)):
            up_copy(step, part).wait_send()

            @pl.when(step < STEPS - 1)
            def _():
                down_copy(step, part).wait_send()

        return carry

    lax.fori_loop(0, STEPS, drain, 0)


def on_device(user_factors, user_rows, row_counts, confidence, slot_items, prev_factors):
    conf = confidence.reshape(WINDOW, DEPTH)
    live = lax.broadcasted_iota(jnp.int32, (WINDOW, DEPTH), 1) < row_counts[:, None]
    conf = jnp.pad(jnp.where(live, conf, jnp.zeros_like(conf)), ((0, 0), (0, 8 - DEPTH)))
    vmem = pl.BlockSpec(memory_space=pltpu.VMEM)
    smem = pl.BlockSpec(memory_space=pltpu.SMEM)
    f32, bf16 = jnp.float32, jnp.bfloat16
    dma = pltpu.SemaphoreType.DMA
    parts, chunks = len(CUTS), len(CHUNKS)
    return pl.pallas_call(
        kernel,
        out_shape=jax.ShapeDtypeStruct((1, 1, RANK), f32),
        in_specs=[smem, smem, vmem, vmem, vmem],
        out_specs=vmem,
        scratch_shapes=[
            pltpu.VMEM((USERS, RANK), f32),
            pltpu.VMEM((PEERS * max(SIZES), RANK), f32),
            pltpu.VMEM((len(CHUNKS), PEERS, max(SIZES), RANK), bf16),
            pltpu.VMEM((len(CHUNKS), PEERS, max(SIZES), RANK), bf16),
            pltpu.VMEM((PEERS * max(SIZES), RANK), f32),
            pltpu.VMEM((WINDOW, RANK), f32),
            pltpu.VMEM((PEERS // 16, 16, RANK), f32),
            pltpu.VMEM((len(CHUNKS), 8, LENGTH), f32),
            pltpu.VMEM((len(CHUNKS), 8, LENGTH), f32),
            pltpu.VMEM((RANK, RANK), f32),
            pltpu.VMEM((PLANE, PIECE, RANK), f32),
            pltpu.VMEM((PLANE, PIECE, RANK), f32),
            pltpu.VMEM((PIECE, RANK), f32),
            pltpu.VMEM((PLANE, PIECE, RANK), f32),
            pltpu.VMEM((3, PIECE, RANK), f32),
            pltpu.VMEM((9, PIECE, RANK), f32),
            pltpu.VMEM((STEPS, UNIT, RANK), f32),
            pltpu.VMEM((STEPS, UNIT, RANK), f32),
            pltpu.VMEM((STEPS, UNIT, RANK), f32),
            pltpu.VMEM((STEPS, UNIT, RANK), f32),
            dma((chunks,)), dma((chunks,)), dma((chunks,)), dma((2,)), dma((2,)), dma((9,)), dma((9,)),
            dma((STEPS, parts)), dma((STEPS, parts)), dma((STEPS, parts)), dma((STEPS, parts)),
        ],
        compiler_params=pltpu.CompilerParams(
            collective_id=0, has_side_effects=True, vmem_limit_bytes=48 * 1024 * 1024
        ),
    )(slot_items, user_rows, conf, user_factors, prev_factors)


def solution(mesh):
    in_specs = (
        P(("grp", "own"), None),
        P(("grp", "own")),
        P(("grp", "own")),
        P(("grp", "own")),
        P(),
        P("own", "grp", None),
    )
    out_specs = P("own", "grp", None)
    return jax.shard_map(
        on_device, mesh=mesh, in_specs=in_specs, out_specs=out_specs, check_vma=False
    )
```

time: 93.6 us -> 87.4 us (0.934)
  the two profiles are of different devices: /device:TPU:6 before, /device:TPU:4 now
where the time goes in v3:
time: 87.4 us; the launch traced here: 87.2 us
  Pallas kernels  84.4 us (97%)
  local copies, waits for them, and re-layouts  2.55 us (3%)
    pallas_call x1, Pallas kernels, on_device(): pl.pallas_call(kernel, out_shape=jax.ShapeDtypeStruct((1, 1, RANK), f32),...  84.4 us

profile of v3, /device:TPU:4, one launch (start us, length us, event | category | flops | bytes accessed | tf_op | source)
XLA Modules:
  0.0 87.2 jit_solution(12796280991557168253)
XLA Ops:
  0.0 0.0 copy-start.4
  0.0 0.0 copy-start
  0.0 1.3 %reshape.4 = bf16[1024,6]{1,0:T(8,128)(2,1)S(1)} reshape(bf16[6144]{0:T(1024)(128)(2,1)} %param.9) | data formatting | bytes 24576 | tf_op jit(solution)/shard_map/reshape | solution.py:424
  1.3 0.0 copy-done.4
  1.3 0.2 fusion
  1.6 0.0 copy-start.1
  1.6 0.0 copy-start.2
  1.6 0.0 copy-start.3
  1.6 0.1 pad.4.conf
  1.7 0.0 copy-done
  1.7 0.6 copy-done.1
  2.3 0.0 copy-done.2
  2.3 0.0 copy-done.3
  2.3 84.4 %shard_map.64 = f32[1,1,128]{2,1,0:T(1,128)S(1)} custom-call(s32[1024]{0:T(1024)S(1)} %copy-done.2, s32[6144]{0:T(1024)S(1)} %copy-done.1, bf16[1024,8]{1,0:T(8,128)(2,1)S(1)} %pad.4.conf, bf16[4096,128]{1,0:T(8,128)(2,1)S(1)} %copy-done, f32[1,1,128]{2,1,0:T(1,128)S(1)} %copy-done.3), custom_call_target="tpu_custom_call" | custom-call | tf_op jit(solution)/shard_map/pallas_call | solution.py:432
  86.7 0.5 copy.8
Async XLA Ops:
  0.0 1.3 %copy-start.4 = (s32[1024]{0:T(1024)S(1)}, s32[1024]{0:T(1024)}, u32[]{:S(2)}) copy-start(s32[1024]{0:T(1024)} %param.8) | copy-start | bytes 12292
  0.0 1.7 %copy-start = (bf16[4096,128]{1,0:T(8,128)(2,1)S(1)}, bf16[4096,128]{1,0:T(8,128)(2,1)}, u32[]{:S(2)}) copy-start(bf16[4096,128]{1,0:T(8,128)(2,1)} %users.1) | copy-start | bytes 3145732
  1.6 0.7 copy-start.1
  1.6 0.7 copy-start.2
  1.6 0.7 copy-start.3

commit v4 on v3

--- a/solution.py
+++ b/solution.py
@@ -21,7 +21,8 @@
 STEPS = ITEMS // 2
 PADDED = 8
 LENGTH = PEERS * PADDED
-CHUNKS = ((0, 1), (1, 3), (4, 4))
+CHUNKS = ((0, 1), (1, 1), (2, 1), (3, 1), (4, 2), (6, 2))
+AHEAD = 2
 SIZES = tuple(2 * steps * PADDED for _, steps in CHUNKS)
 UNIT = RANK + 8
 CUTS = ((0, 64), (64, 72))
@@ -356,10 +357,9 @@
     post_rows(0)
     own_gram()
     post_gram()
-    gather(1)
-    post_rows(1)
-    gather(2)
-    post_rows(2)
+    for chunk in range(1, AHEAD):
+        gather(chunk)
+        post_rows(chunk)
 
     def chain(step, chunk):
         index = (step - CHUNKS[chunk][0]) * 2
@@ -376,6 +376,9 @@
                 down_send[step, at] += down_recv[step - 1, at]
             if step < STEPS - 1:
                 down_copy(step, part).start()
+        if AHEAD + step < len(CHUNKS):
+            gather(AHEAD + step)
+            post_rows(AHEAD + step)
         beside(step)
 
     for chunk, (first, count) in enumerate(CHUNKS):

time: 87.4 us -> 78.8 us (0.902)
  the two profiles are of different devices: /device:TPU:4 before, /device:TPU:6 now
where the time goes in v4:
time: 78.8 us; the launch traced here: 77.5 us
  Pallas kernels  74.7 us (95%)
  local copies, waits for them, and re-layouts  2.55 us (3%)
    pallas_call x1, Pallas kernels, on_device(): pl.pallas_call(kernel, out_shape=jax.ShapeDtypeStruct((1, 1, RANK), f32),...  74.7 us

profile of v4, /device:TPU:6, one launch (start us, length us, event | category | flops | bytes accessed | tf_op | source)
XLA Modules:
  0.0 77.5 jit_solution(17914486232361138808)
XLA Ops:
  0.0 0.0 copy-start.4
  0.0 0.0 copy-start
  0.0 1.3 %reshape.4 = bf16[1024,6]{1,0:T(8,128)(2,1)S(1)} reshape(bf16[6144]{0:T(1024)(128)(2,1)} %param.9) | data formatting | bytes 24576 | tf_op jit(solution)/shard_map/reshape | solution.py:427
  1.3 0.0 copy-done.4
  1.3 0.2 fusion
  1.6 0.0 copy-start.1
  1.6 0.0 copy-start.2
  1.6 0.0 copy-start.3
  1.6 0.1 pad.4.conf
  1.7 0.0 copy-done
  1.7 0.6 copy-done.1
  2.3 0.0 copy-done.2
  2.3 0.0 copy-done.3
  2.3 74.7 %shard_map.64 = f32[1,1,128]{2,1,0:T(1,128)S(1)} custom-call(s32[1024]{0:T(1024)S(1)} %copy-done.2, s32[6144]{0:T(1024)S(1)} %copy-done.1, bf16[1024,8]{1,0:T(8,128)(2,1)S(1)} %pad.4.conf, bf16[4096,128]{1,0:T(8,128)(2,1)S(1)} %copy-done, f32[1,1,128]{2,1,0:T(1,128)S(1)} %copy-done.3), custom_call_target="tpu_custom_call" | custom-call | tf_op jit(solution)/shard_map/pallas_call | solution.py:435
  77.0 0.5 copy.8
Async XLA Ops:
  0.0 1.3 %copy-start.4 = (s32[1024]{0:T(1024)S(1)}, s32[1024]{0:T(1024)}, u32[]{:S(2)}) copy-start(s32[1024]{0:T(1024)} %param.8) | copy-start | bytes 12292
  0.0 1.7 %copy-start = (bf16[4096,128]{1,0:T(8,128)(2,1)S(1)}, bf16[4096,128]{1,0:T(8,128)(2,1)}, u32[]{:S(2)}) copy-start(bf16[4096,128]{1,0:T(8,128)(2,1)} %users.1) | copy-start | bytes 3145732
  1.6 0.7 copy-start.1
  1.6 0.7 copy-start.2
  1.6 0.7 copy-start.3

commit v5 on v4

--- a/solution.py
+++ b/solution.py
@@ -130,21 +130,23 @@
 
     lax.fori_loop(0, USERS // 512, widen_users, 0)
 
-    def item_of(base, d, index):
+    def slots_of(base, index):
         step = index // 2
         away = STEPS - step if index % 2 == 0 else step - (STEPS - 1)
-        return items[wrapped(base + 2 * away, PLANES) * PLANE + d]
-
-    def each_receiver(act):
+        return wrapped(base + 2 * away, PLANES) * PLANE
+
+    def each_receiver(first, count, act):
         for far in range(2):
             for pc in range(2):
                 base = far_planes[pc] if far else z
-
-                def one(grp, carry):
-                    act(far * PLANE + pc * 16 + grp, pc * 16 + grp, base)
+                begins = [slots_of(base, first + index) for index in range(count)]
+
+                def two(pair, carry):
+                    for grp in (2 * pair, 2 * pair + 1):
+                        act(far * PLANE + pc * 16 + grp, pc * 16 + grp, begins)
                     return carry
 
-                lax.fori_loop(0, 16, one, 0)
+                lax.fori_loop(0, 8, two, 0)
 
     def spread_conf():
         spread_row = lax.broadcasted_iota(jnp.int32, (8, RANK), 0)
@@ -157,15 +159,15 @@
         first, count = CHUNKS[chunk]
         group, size = 2 * count, SIZES[chunk]
 
-        def owner(to, d, base):
+        def owner(to, d, begins):
             for index in range(group):
-                item = item_of(base, d, 2 * first + index)
+                item = items[begins[index] + d]
                 for slot in range(DEPTH):
                     row = rows[item * DEPTH + slot]
                     stage[pl.ds(to * size + slot * group + index, 1), :] = wide[pl.ds(row, 1), :]
                 stage[pl.ds(to * size + DEPTH * group + index, 1), :] = conf_wide[pl.ds(item, 1), :]
 
-        each_receiver(owner)
+        each_receiver(2 * first, group, owner)
 
         def narrow(block, carry):
             at = pl.ds(pl.multiple_of(block * size * 4, size * 4), size * 4)
@@ -216,13 +218,12 @@
         live = lax.broadcasted_iota(jnp.int32, (size, RANK), 0) < used
 
         def sixteen(part, carry):
-            def widen(index, total):
+            total = jnp.zeros((size - tail, RANK), jnp.float32)
+            for index in range(16):
                 source = part * 16 + index
                 block = recv[chunk, source, pl.ds(0, size)].astype(jnp.float32)
                 flat[pl.ds(pl.multiple_of(source * size, size), size), :] = jnp.where(live, block, 0.0)
-                return total + block[tail:]
-
-            total = lax.fori_loop(0, 16, widen, jnp.zeros((size - tail, RANK), jnp.float32))
+                total = total + block[tail:]
             conf_parts[part, pl.ds(0, size - tail)] = total
             return carry
 

time: 78.8 us -> 78.6 us (level)
  the two profiles are of different devices: /device:TPU:6 before, /device:TPU:7 now
where the time goes in v5:
time: 78.6 us; the launch traced here: 78.4 us
  Pallas kernels  75.5 us (96%)
  local copies, waits for them, and re-layouts  2.55 us (3%)
    pallas_call x1, Pallas kernels, on_device(): pl.pallas_call(kernel, out_shape=jax.ShapeDtypeStruct((1, 1, RANK), f32),...  75.5 us

profile of v5, /device:TPU:7, one launch (start us, length us, event | category | flops | bytes accessed | tf_op | source)
XLA Modules:
  0.0 78.4 jit_solution(6836171608736000901)
XLA Ops:
  0.0 0.0 copy-start.4
  0.0 0.0 copy-start
  0.0 1.3 %reshape.4 = bf16[1024,6]{1,0:T(8,128)(2,1)S(1)} reshape(bf16[6144]{0:T(1024)(128)(2,1)} %param.9) | data formatting | bytes 24576 | tf_op jit(solution)/shard_map/reshape | solution.py:428
  1.3 0.0 copy-done.4
  1.3 0.2 fusion
  1.6 0.0 copy-start.1
  1.6 0.0 copy-start.2
  1.6 0.0 copy-start.3
  1.6 0.1 pad.4.conf
  1.7 0.0 copy-done
  1.7 0.6 copy-done.1
  2.3 0.0 copy-done.2
  2.3 0.0 copy-done.3
  2.3 75.5 %shard_map.64 = f32[1,1,128]{2,1,0:T(1,128)S(1)} custom-call(s32[1024]{0:T(1024)S(1)} %copy-done.2, s32[6144]{0:T(1024)S(1)} %copy-done.1, bf16[1024,8]{1,0:T(8,128)(2,1)S(1)} %pad.4.conf, bf16[4096,128]{1,0:T(8,128)(2,1)S(1)} %copy-done, f32[1,1,128]{2,1,0:T(1,128)S(1)} %copy-done.3), custom_call_target="tpu_custom_call" | custom-call | tf_op jit(solution)/shard_map/pallas_call | solution.py:436
  77.8 0.5 copy.8
Async XLA Ops:
  0.0 1.3 %copy-start.4 = (s32[1024]{0:T(1024)S(1)}, s32[1024]{0:T(1024)}, u32[]{:S(2)}) copy-start(s32[1024]{0:T(1024)} %param.8) | copy-start | bytes 12292
  0.0 1.7 %copy-start = (bf16[4096,128]{1,0:T(8,128)(2,1)S(1)}, bf16[4096,128]{1,0:T(8,128)(2,1)}, u32[]{:S(2)}) copy-start(bf16[4096,128]{1,0:T(8,128)(2,1)} %users.1) | copy-start | bytes 3145732
  1.6 0.7 copy-start.1
  1.6 0.7 copy-start.2
  1.6 0.7 copy-start.3
